TPU v7x, 128 devices: a whole 4x4x4 slice. The times are simulated.
128 devices in a mesh: head: 4 (over x), expert: 16 (over y, z_hi, core), dp: 2 (over z_lo).
Axes of the slice: x: 4, y: 4, z: 4 (z_hi: 2, z_lo: 2; z = z_hi * 2 + z_lo), core: 2. Of those that a mesh axis runs over, the one named last changes fastest.
Arguments:
- tokens: bfloat16 [32, 1024, 768], P(('expert', 'dp'), 'head'), may hold values from -6 to 6
- out_grad: bfloat16 [32, 1024, 768], P(('expert', 'dp'), 'head'), may hold values from -6 to 6
- w_query: bfloat16 [768, 768], P(None, 'head'), may hold values from -0.21875 to 0.21875
- w_key: bfloat16 [768, 768], P(None, 'head'), may hold values from -0.21875 to 0.21875
- w_value: bfloat16 [768, 768], P(None, 'head'), may hold values from -0.21875 to 0.21875
- w_output: bfloat16 [768, 768], P('head'), may hold values from -0.875 to 0.875
- gain_one: float32 [768], replicated, may hold values from 0.5 to 1.5
- gain_two: float32 [768], replicated, may hold values from 0.5 to 1.5
- expert_up: bfloat16 [16, 768, 3072], P('expert'), may hold values from -0.21875 to 0.21875
- expert_down: bfloat16 [16, 3072, 768], P('expert'), may hold values from -0.109375 to 0.109375
- hash_table: int32 [32768], replicated, may hold values from 0 to 15, as said below
- token_ids: int32 [32, 1024], P(('expert', 'dp'), 'head'), may hold values from 0 to 32767, as said below
- doc_lengths: int32 [32, 8], P(('expert', 'dp')), may hold values from 1 to 256, 1024 in all within a row
- turn_mask: int32 [32, 1024], P(('expert', 'dp')), may hold values 0 or 1
Outputs:
- final: float32 [32, 1024, 768], P(('expert', 'dp'), 'head')
- tokens_grad: float32 [32, 1024, 768], P(('expert', 'dp'), 'head')
- w_query_grad: float32 [768, 768], P(None, 'head')
- w_key_grad: float32 [768, 768], P(None, 'head')
- w_value_grad: float32 [768, 768], P(None, 'head')
- w_output_grad: float32 [768, 768], P('head')
- gain_one_grad: float32 [768], replicated
- gain_two_grad: float32 [768], replicated
- expert_up_grad: float32 [16, 768, 3072], P('expert')
- expert_down_grad: float32 [16, 3072, 768], P('expert')
- expert_loads: int32 [16], replicated
Inputs may be any that keep to these rules, and one draw needn't show every extreme that they name: hash_table[v] is the expert of token id v; every expert has 2048 ids. `token_ids`: cut each packed row into 4 aligned blocks of 256 tokens. Among the tokens of one block at most 32 have the same expert (through hash_table). For each block position b and each c < 2, one expert, drawn from the seed, has exactly 32 tokens in block b of every packed row whose index is c modulo 2. `doc_lengths`: each row sums to 1024 and its largest entry is 256.
All inputs are finite; a program needn't handle non-finite values. No bound on the sum of `turn_mask` on one device may be relied on, other than what follows from the above.
Results may differ from a plain program's by a relative error of at most 0.02.
Values may be sent and summed in bfloat16 or wider, within the bound.
A program may use at most 128 MiB of HBM per device.

v0:
```python
import jax
import jax.numpy as jnp
from jax import lax
from jax.sharding import PartitionSpec as P

HEAD_DIM = 64


EPSILON = 1e-05
NEGATIVE = -1e30
CONTRACT_ROWS = (((0,), (0,)), ((), ()))
CONTRACT_COLUMNS = (((1,), (1,)), ((), ()))


def norm_rows(values, scales):
    average = jnp.mean(values, axis=-1, keepdims=True)
    centred = values - average
    variance = jnp.mean(centred * centred, axis=-1, keepdims=True)
    return centred * lax.rsqrt(variance + EPSILON) * scales


def doc_ids(doc_lengths, length):
    endings = jnp.cumsum(doc_lengths)
    places = jnp.arange(length, dtype=jnp.int32)
    return jnp.sum((endings[None, :] <= places[:, None]).astype(jnp.int32), axis=1)


def masked_scores(queries, keys_all, first_row, segments, prompt, factor):
    height = queries.shape[0]
    scores = (
        jnp.einsum("qhd,khd->hqk", queries, keys_all, preferred_element_type=jnp.float32) * factor
    )
    query_pos = first_row + jnp.arange(height, dtype=jnp.int32)
    key_pos = jnp.arange(keys_all.shape[0], dtype=jnp.int32)
    query_seg = segments[first_row : first_row + height]
    allowed = (query_seg[:, None] == segments[None, :]) & (
        (key_pos[None, :] <= query_pos[:, None]) | (prompt[None, :] == 1)
    )
    return jnp.where(allowed[None], scores, NEGATIVE)


def body(
    tokens,
    out_grad,
    w_query,
    w_key,
    w_value,
    w_output,
    gain_one,
    gain_two,
    expert_up,
    expert_down,
    hash_table,
    token_ids,
    doc_lengths,
    turn_mask,
):
    local_rows = tokens.shape[1]
    width = tokens.shape[2]
    row_length = local_rows * lax.axis_size("head")
    expert_count = lax.axis_size("expert")
    capacity = 2 * local_rows // expert_count
    head_cols = w_query.shape[1]
    head_count = head_cols // HEAD_DIM
    factor = HEAD_DIM ** (-0.5)
    span_rows = min(512, row_length)
    starts = list(range(0, row_length, span_rows))
    segments = doc_ids(doc_lengths[0], row_length)
    prompt = turn_mask[0]
    residual = tokens[0].astype(jnp.float32)
    normed_one, pull_one = jax.vjp(norm_rows, residual, gain_one)
    gathered = lax.all_gather(normed_one.astype(jnp.bfloat16), "head", axis=0, tiled=True)
    w_joint = jnp.concatenate([w_query, w_key, w_value], axis=1)
    joint = jnp.dot(gathered, w_joint, preferred_element_type=jnp.float32).astype(jnp.bfloat16)
    queries = joint[:, :head_cols].reshape(row_length, head_count, HEAD_DIM)
    keys_all = joint[:, head_cols : 2 * head_cols].reshape(row_length, head_count, HEAD_DIM)
    values_all = joint[:, 2 * head_cols :].reshape(row_length, head_count, HEAD_DIM)
    pieces = []
    log_sums = []
    for first_row in starts:
        scores = masked_scores(
            queries[first_row : first_row + span_rows],
            keys_all,
            first_row,
            segments,
            prompt,
            factor,
        )
        highest = jnp.max(scores, axis=-1, keepdims=True)
        powers = jnp.exp(scores - highest)
        totals = jnp.sum(powers, axis=-1, keepdims=True)
        weights = (powers / totals).astype(jnp.bfloat16)
        pieces.append(
            jnp.einsum(
                "hqk,khd->qhd", weights, values_all, preferred_element_type=jnp.float32
            ).astype(jnp.bfloat16)
        )
        log_sums.append(highest + jnp.log(totals))
    attended = jnp.concatenate(pieces, axis=0).reshape(row_length, head_cols)
    section = attended
    mixed = lax.psum_scatter(
        jnp.dot(section, w_output, preferred_element_type=jnp.float32),
        "head",
        scatter_dimension=0,
        tiled=True,
    )
    hidden = residual + mixed
    normed_two, pull_two = jax.vjp(norm_rows, hidden, gain_two)
    chosen = jnp.take(hash_table, token_ids[0])
    one_hot = (chosen[:, None] == jnp.arange(expert_count, dtype=jnp.int32)[None, :]).astype(
        jnp.int32
    )
    arrival = jnp.sum(jnp.cumsum(one_hot, axis=0) * one_hot, axis=1) - 1
    slots = chosen * capacity + arrival
    local_loads = jnp.sum(one_hot, axis=0).astype(jnp.float32)

    def to_slots(row_values):
        empty = jnp.zeros((expert_count * capacity, width), row_values.dtype)
        return empty.at[slots].set(row_values).reshape(expert_count, capacity, width)

    arrived = lax.all_to_all(
        to_slots(normed_two.astype(jnp.bfloat16)), "expert", split_axis=0, concat_axis=0, tiled=True
    )
    slot_rows = arrived.reshape(expert_count * capacity, width)
    up_weight = expert_up[0]
    down_weight = expert_down[0]
    before = jnp.dot(slot_rows, up_weight, preferred_element_type=jnp.float32)
    active_full, gelu_pull = jax.vjp(jax.nn.gelu, before)
    active = active_full.astype(jnp.bfloat16)
    produced = jnp.dot(active, down_weight, preferred_element_type=jnp.float32).astype(jnp.bfloat16)
    returned = lax.all_to_all(
        produced.reshape(expert_count, capacity, width),
        "expert",
        split_axis=0,
        concat_axis=0,
        tiled=True,
    )
    branch_out = returned.reshape(expert_count * capacity, width)[slots].astype(jnp.float32)
    final = hidden + branch_out
    grad_final = out_grad[0]
    grad_slots = lax.all_to_all(
        to_slots(grad_final), "expert", split_axis=0, concat_axis=0, tiled=True
    ).reshape(expert_count * capacity, width)
    again_before = jnp.dot(slot_rows, up_weight, preferred_element_type=jnp.float32)
    again_active, act_pull = jax.vjp(jax.nn.gelu, again_before)
    act_rows = again_active.astype(jnp.bfloat16)
    down_grad = lax.dot_general(
        act_rows, grad_slots, CONTRACT_ROWS, preferred_element_type=jnp.float32
    )
    act_grad = lax.dot_general(
        grad_slots, down_weight, CONTRACT_COLUMNS, preferred_element_type=jnp.float32
    )
    before_grad = act_pull(act_grad)[0].astype(jnp.bfloat16)
    up_grad = lax.dot_general(
        slot_rows, before_grad, CONTRACT_ROWS, preferred_element_type=jnp.float32
    )
    slot_grad = lax.dot_general(
        before_grad, up_weight, CONTRACT_COLUMNS, preferred_element_type=jnp.float32
    ).astype(jnp.bfloat16)
    up_grad, down_grad = (
        lax.psum(up_grad.astype(jnp.bfloat16), ("head", "dp")).astype(jnp.float32),
        lax.psum(down_grad.astype(jnp.bfloat16), ("head", "dp")).astype(jnp.float32),
    )
    sent_back = lax.all_to_all(
        slot_grad.reshape(expert_count, capacity, width),
        "expert",
        split_axis=0,
        concat_axis=0,
        tiled=True,
    )
    normed_two_grad = sent_back.reshape(expert_count * capacity, width)[slots].astype(jnp.float32)
    hidden_part, gain_two_grad = pull_two(normed_two_grad)
    hidden_grad = grad_final.astype(jnp.float32) + hidden_part
    mixed_rows = lax.all_gather(hidden_grad.astype(jnp.bfloat16), "head", axis=0, tiled=True)
    output_grad = lax.dot_general(
        attended, mixed_rows, CONTRACT_ROWS, preferred_element_type=jnp.float32
    )
    attended_grad = lax.dot_general(
        mixed_rows, w_output, CONTRACT_COLUMNS, preferred_element_type=jnp.float32
    )
    attended_grad = attended_grad.astype(jnp.bfloat16).reshape(row_length, head_count, HEAD_DIM)
    query_grads = []
    key_grad = jnp.zeros((row_length, head_count, HEAD_DIM), jnp.float32)
    value_grad = jnp.zeros((row_length, head_count, HEAD_DIM), jnp.float32)
    for position, first_row in enumerate(starts):
        query_rows = queries[first_row : first_row + span_rows]
        scores = masked_scores(query_rows, keys_all, first_row, segments, prompt, factor)
        chances = jnp.exp(scores - log_sums[position])
        upstream = attended_grad[first_row : first_row + span_rows]
        chance_grad = jnp.einsum(
            "qhd,khd->hqk", upstream, values_all, preferred_element_type=jnp.float32
        )
        score_grad = (
            chances * (chance_grad - jnp.sum(chance_grad * chances, axis=-1, keepdims=True))
        ).astype(jnp.bfloat16)
        query_grads.append(
            jnp.einsum("hqk,khd->qhd", score_grad, keys_all, preferred_element_type=jnp.float32)
            * factor
        )
        key_grad = (
            key_grad
            + jnp.einsum("hqk,qhd->khd", score_grad, query_rows, preferred_element_type=jnp.float32)
            * factor
        )
        value_grad = value_grad + jnp.einsum(
            "hqk,qhd->khd",
            chances.astype(jnp.bfloat16),
            upstream,
            preferred_element_type=jnp.float32,
        )
    joint_grad = jnp.concatenate(
        [
            jnp.concatenate(query_grads, axis=0).reshape(row_length, head_cols),
            key_grad.reshape(row_length, head_cols),
            value_grad.reshape(row_length, head_cols),
        ],
        axis=1,
    ).astype(jnp.bfloat16)
    joint_weight_grad = lax.dot_general(
        gathered, joint_grad, CONTRACT_ROWS, preferred_element_type=jnp.float32
    )
    section = joint_grad
    normed_one_grad = lax.psum_scatter(
        lax.dot_general(
            section, w_joint, CONTRACT_COLUMNS, preferred_element_type=jnp.float32
        ).astype(jnp.bfloat16),
        "head",
        scatter_dimension=0,
        tiled=True,
    ).astype(jnp.float32)
    residual_part, gain_one_grad = pull_one(normed_one_grad)
    tokens_grad = hidden_grad + residual_part
    joint_weight_grad, output_grad = (
        lax.psum(joint_weight_grad.astype(jnp.bfloat16), ("expert", "dp")).astype(jnp.float32),
        lax.psum(output_grad.astype(jnp.bfloat16), ("expert", "dp")).astype(jnp.float32),
    )
    gain_one_grad, gain_two_grad, all_loads = lax.psum(
        (gain_one_grad, gain_two_grad, local_loads), ("head", "expert", "dp")
    )
    return (
        final[None],
        tokens_grad[None],
        joint_weight_grad[:, :head_cols],
        joint_weight_grad[:, head_cols : 2 * head_cols],
        joint_weight_grad[:, 2 * head_cols :],
        output_grad,
        gain_one_grad,
        gain_two_grad,
        up_grad[None],
        down_grad[None],
        all_loads.astype(jnp.int32),
    )


def solution(mesh):
    in_specs = (
        P(("expert", "dp"), "head", None),
        P(("expert", "dp"), "head", None),
        P(None, "head"),
        P(None, "head"),
        P(None, "head"),
        P("head", None),
        P(),
        P(),
        P("expert", None, None),
        P("expert", None, None),
        P(),
        P(("expert", "dp"), "head"),
        P(("expert", "dp"), None),
        P(("expert", "dp"), None),
    )
    out_specs = (
        P(("expert", "dp"), "head", None),
        P(("expert", "dp"), "head", None),
        P(None, "head"),
        P(None, "head"),
        P(None, "head"),
        P("head", None),
        P(),
        P(),
        P("expert", None, None),
        P("expert", None, None),
        P(),
    )
    return jax.shard_map(body, mesh=mesh, in_specs=in_specs, out_specs=out_specs, check_vma=False)
```

profile of v0, /device:TPU:80, one launch (start us, length us, event | category | flops | bytes accessed | tf_op | source)
XLA Modules:
  0.0 778.8 jit_solution(678730269815860745)
XLA Ops:
  18.6 21.2 %all-gather.3.cloned.1.call-done = bf16[1024,768]{1,0:T(8,128)(2,1)} async-done(((bf16[256,768]{1,0:T(8,128)(2,1)}), bf16[1024,768]{1,0:T(8,128)(2,1)}) %all-gather.3.cloned.1.call-update) | async-done | bytes 1572880 | tf_op jit(solution)/shard_map/all_gather | solution.py:72
  39.8 2.7 convolution_convert_fusion.3
  52.1 2.3 fusion.100
  57.3 35.7 %reduce-scatter.3.cloned.1.call-done = f32[256,768]{1,0:T(8,128)} async-done(((f32[1024,768]{1,0:T(8,128)}), f32[256,768]{1,0:T(8,128)}) %reduce-scatter.3.cloned.1.call-update) | async-done | bytes 786448 | tf_op jit(solution)/shard_map/reduce_scatter | solution.py:101
  94.5 2.7 scatter_custom_fusion
  97.2 7.5 all-to-all-start
  104.7 2.6 scatter_custom_fusion.1
  107.2 8.1 %all-to-all-done = bf16[16,32,768]{2,1,0:T(8,128)(2,1)S(1)} async-done(((bf16[16,32,768]{2,1,0:T(8,128)(2,1)}), bf16[16,32,768]{2,1,0:T(8,128)(2,1)S(1)}, u32[]{:S(2)}, u32[]{:S(2)}) %all-to-all-start) | async-done | bytes 786464 | tf_op jit(solution)/shard_map/all_to_all | solution.py:121
  115.3 8.0 %all-to-all-start.2 = ((bf16[16,32,768]{2,1,0:T(8,128)(2,1)}), bf16[16,32,768]{2,1,0:T(8,128)(2,1)S(1)}, u32[]{:S(2)}, u32[]{:S(2)}) async-start(bf16[16,32,768]{2,1,0:T(8,128)(2,1)} %bitcast.27), calls=%async_computation.3 | async-start | bytes 1572864 | tf_op jit(solution)/shard_map/all_to_all | solution.py:141
  123.3 6.8 fusion.17
  130.1 3.9 all-to-all-done.2
  134.0 8.9 %fusion.6 = bf16[512,3072]{1,0:T(8,128)(2,1)S(1)} fusion(f32[512,3072]{1,0:T(8,128)} %fusion.17, bf16[512,768]{1,0:T(8,128)(2,1)S(1)} %bitcast.183, bf16[1,3072,768]{2,1,0:T(8,128)(2,1)} %param.23), kind=kOutput, calls=%fused_computation.13 | convolution fusion | flops 2447376384 | bytes 14942208 | tf_op jit(solution)/shard_map/dot_general | solution.py:150
  142.9 7.0 fusion.35
  149.9 8.0 %all-to-all-start.3 = ((bf16[16,32,768]{2,1,0:T(8,128)(2,1)}), bf16[16,32,768]{2,1,0:T(8,128)(2,1)S(1)}, u32[]{:S(2)}, u32[]{:S(2)}) async-start(bf16[16,32,768]{2,1,0:T(8,128)(2,1)} %bitcast.186), calls=%async_computation.4 | async-start | bytes 1572864 | tf_op jit(solution)/shard_map/all_to_all | solution.py:164
  157.9 8.8 %fusion.38 = bf16[512,768]{1,0:T(8,128)(2,1)} fusion(bf16[1,3072,768]{2,1,0:T(8,128)(2,1)} %param.23, f32[512,3072]{1,0:T(8,128)} %fusion.17), kind=kOutput, calls=%fused_computation.59 | convolution fusion | flops 2430468096 | bytes 11796480 | tf_op jit(solution)/shard_map/dot_general | solution.py:130
  168.7 8.0 %all-to-all-start.1 = ((bf16[16,32,768]{2,1,0:T(8,128)(2,1)}), bf16[16,32,768]{2,1,0:T(8,128)(2,1)S(1)}, u32[]{:S(2)}, u32[]{:S(2)}) async-start(bf16[16,32,768]{2,1,0:T(8,128)(2,1)} %bitcast.185), calls=%async_computation.2 | async-start | bytes 1572864 | tf_op jit(solution)/shard_map/all_to_all | solution.py:131
  178.6 8.9 %all-to-all-done.1 = bf16[16,32,768]{2,1,0:T(8,128)(2,1)S(1)} async-done(((bf16[16,32,768]{2,1,0:T(8,128)(2,1)}), bf16[16,32,768]{2,1,0:T(8,128)(2,1)S(1)}, u32[]{:S(2)}, u32[]{:S(2)}) %all-to-all-start.1) | async-done | bytes 786464 | tf_op jit(solution)/shard_map/all_to_all | solution.py:131
  189.4 2.4 fusion.90
  194.7 26.3 %all-gather.5.cloned.1.call-done = bf16[1024,768]{1,0:T(8,128)(2,1)} async-done(((bf16[256,768]{1,0:T(8,128)(2,1)}), bf16[1024,768]{1,0:T(8,128)(2,1)}) %all-gather.5.cloned.1.call-update) | async-done | bytes 1572880 | tf_op jit(solution)/shard_map/all_gather | solution.py:174
  223.1 4.1 fusion.21
  227.3 2.9 multiply_reduce_fusion
  243.4 3.6 convolution_convert_fusion.2
  247.1 6.2 fusion.19
  253.3 8.4 %fusion.20 = bf16[1,3072,768]{2,1,0:T(8,128)(2,1)} fusion(bf16[512,768]{1,0:T(8,128)(2,1)S(1)} %bitcast.184, f32[512,3072]{1,0:T(8,128)} %fusion.17), kind=kOutput, calls=%fused_computation.42 | convolution fusion | flops 2432434176 | bytes 11796480 | tf_op jit(solution)/shard_map/dot_general | solution.py:147
  261.7 83.4 %all-reduce.6.cloned.1.call-done = (bf16[768,576]{0,1:T(8,128)(2,1)}, bf16[192,768]{1,0:T(8,128)(2,1)}) async-done(((bf16[768,576]{0,1:T(8,128)(2,1)}, bf16[192,768]{1,0:T(8,128)(2,1)}), (bf16[768,576]{0,1:T(8,128)(2,1)}, bf16[192,768]{1,0:T(8,128)(2,1)})) %all-reduce.6.cloned.1.call-update) | async-done | bytes 1179664 | tf_op jit(solution)/shard_map/psum | solution.py:234
  346.9 2.4 fusion.95
  349.3 26.8 %reduce-scatter.5.cloned.1.call-done = bf16[256,768]{1,0:T(8,128)(2,1)} async-done(((bf16[1024,768]{1,0:T(8,128)(2,1)}), bf16[256,768]{1,0:T(8,128)(2,1)}) %reduce-scatter.5.cloned.1.call-update) | async-done | bytes 393232 | tf_op jit(solution)/shard_map/reduce_scatter | solution.py:223
  378.9 100.5 %all-reduce = (f32[768]{0:T(1024)}, f32[768]{0:T(1024)}, f32[16]{0:T(128)S(1)}) all-reduce(f32[768]{0:T(1024)S(1)} %get-tuple-element.13, f32[768]{0:T(1024)S(1)} %get-tuple-element.11, f32[16]{0:T(128)S(1)} %convert_element_type.151), channel_id=1, replica_groups=mesh['head'=4,'expert'=16,'dp'=2] {'head','expert','dp'}, use_global_device_ids=true, to_apply=%region_26.27 | all-reduce | flops 1552 | bytes 12416 | tf_op jit(solution)/shard_map/psum | solution.py:237
  480.0 2.3 add_bitcast_fusion
  482.2 277.3 %all-reduce.8.cloned.1.call-done = (bf16[1,768,3072]{2,1,0:T(8,128)(2,1)}, bf16[1,3072,768]{2,1,0:T(8,128)(2,1)}) async-done(((bf16[1,768,3072]{2,1,0:T(8,128)(2,1)}, bf16[1,3072,768]{2,1,0:T(8,128)(2,1)}), (bf16[1,768,3072]{2,1,0:T(8,128)(2,1)}, bf16[1,3072,768]{2,1,0:T(8,128)(2,1)})) %all-reduce.8.cloned.1.call-update) | async-done | bytes 9437200 | tf_op jit(solution)/shard_map/psum | solution.py:161
  759.5 7.5 broadcast_in_dim.119
  767.1 4.5 broadcast_in_dim.121
  (159 shorter events, 54.1 us)
Async XLA Ops:
  7.2 44.9 %copy-start = (bf16[192,768]{1,0:T(8,128)(2,1)S(1)}, bf16[192,768]{1,0:T(8,128)(2,1)}, u32[]{:S(2)}) copy-start(bf16[192,768]{1,0:T(8,128)(2,1)} %param.19) | copy-start | bytes 884740
  7.2 32.6 %all-gather.3.cloned.1.call-start = ((), (), s32[]{:S(2)}) async-start(), calls=%async_computation.6 | async-start | bytes 1966080 | tf_op jit(solution)/shard_map/all_gather | solution.py:72
  11.7 81.3 %reduce-scatter.3.cloned.1.call-start = ((), (), s32[]{:S(2)}) async-start(), calls=%async_computation.7 | async-start | bytes 3932160 | tf_op jit(solution)/shard_map/reduce_scatter | solution.py:101
  42.6 4.7 copy-start.6
  42.6 7.7 copy-start.12
  42.7 4.7 copy-start.21
  52.0 40.9 %copy-start.4 = (bf16[1,256,768]{2,1,0:T(8,128)(2,1)S(1)}, bf16[1,256,768]{2,1,0:T(8,128)(2,1)}, u32[]{:S(2)}) copy-start(bf16[1,256,768]{2,1,0:T(8,128)(2,1)} %param.14) | copy-start | bytes 1179652
  52.1 42.4 %copy-start.30 = (f32[768]{0:T(1024)S(1)}, f32[768]{0:T(1024)}, u32[]{:S(2)}) copy-start(f32[768]{0:T(1024)} %param.21) | copy-start | bytes 9220
  52.1 5.1 copy-start.16
  52.1 52.5 %copy-start.14 = (bf16[1,256,768]{2,1,0:T(8,128)(2,1)S(1)}, bf16[1,256,768]{2,1,0:T(8,128)(2,1)}, u32[]{:S(2)}) copy-start(bf16[1,256,768]{2,1,0:T(8,128)(2,1)} %param.15) | copy-start | bytes 1179652
  97.2 18.1 %all-to-all-start = ((bf16[16,32,768]{2,1,0:T(8,128)(2,1)}), bf16[16,32,768]{2,1,0:T(8,128)(2,1)S(1)}, u32[]{:S(2)}, u32[]{:S(2)}) async-start(bf16[16,32,768]{2,1,0:T(8,128)(2,1)} %bitcast.19), calls=%async_computation.1 | async-start | bytes 1572864 | tf_op jit(solution)/shard_map/all_to_all | solution.py:121
  115.3 14.8 %copy-start.19 = (bf16[16,32,768]{2,1,0:T(8,128)(2,1)}, bf16[16,32,768]{2,1,0:T(8,128)(2,1)S(1)}, u32[]{:S(2)}) copy-start(bf16[16,32,768]{2,1,0:T(8,128)(2,1)S(1)} %all-to-all-done) | copy-start | bytes 2359300
  115.3 18.7 %all-to-all-start.2 = ((bf16[16,32,768]{2,1,0:T(8,128)(2,1)}), bf16[16,32,768]{2,1,0:T(8,128)(2,1)S(1)}, u32[]{:S(2)}, u32[]{:S(2)}) async-start(bf16[16,32,768]{2,1,0:T(8,128)(2,1)} %bitcast.27), calls=%async_computation.3 | async-start | bytes 1572864 | tf_op jit(solution)/shard_map/all_to_all | solution.py:141
  134.0 8.9 %copy-start.24 = (bf16[16,32,768]{2,1,0:T(8,128)(2,1)}, bf16[16,32,768]{2,1,0:T(8,128)(2,1)S(1)}, u32[]{:S(2)}) copy-start(bf16[16,32,768]{2,1,0:T(8,128)(2,1)S(1)} %all-to-all-done.2) | copy-start | bytes 2359300
  142.9 7.0 copy-start.33
  149.9 18.8 %all-to-all-start.3 = ((bf16[16,32,768]{2,1,0:T(8,128)(2,1)}), bf16[16,32,768]{2,1,0:T(8,128)(2,1)S(1)}, u32[]{:S(2)}, u32[]{:S(2)}) async-start(bf16[16,32,768]{2,1,0:T(8,128)(2,1)} %bitcast.186), calls=%async_computation.4 | async-start | bytes 1572864 | tf_op jit(solution)/shard_map/all_to_all | solution.py:164
  168.7 18.8 %all-to-all-start.1 = ((bf16[16,32,768]{2,1,0:T(8,128)(2,1)}), bf16[16,32,768]{2,1,0:T(8,128)(2,1)S(1)}, u32[]{:S(2)}, u32[]{:S(2)}) async-start(bf16[16,32,768]{2,1,0:T(8,128)(2,1)} %bitcast.185), calls=%async_computation.2 | async-start | bytes 1572864 | tf_op jit(solution)/shard_map/all_to_all | solution.py:131
  176.7 44.3 %all-gather.5.cloned.1.call-start = ((), (), s32[]{:S(2)}) async-start(), calls=%async_computation.8 | async-start | bytes 1966080 | tf_op jit(solution)/shard_map/all_gather | solution.py:174
  178.2 9.3 %copy-start.18 = (bf16[256,768]{1,0:T(8,128)(2,1)}, bf16[256,768]{1,0:T(8,128)(2,1)S(1)}, u32[]{:S(2)}) copy-start(bf16[256,768]{1,0:T(8,128)(2,1)S(1)} %gather_fusion.2) | copy-start | bytes 1179652
  189.4 37.9 %slice-start.2 = ((s8[6291456]{0:T(1024)(128)(4,1)}), s8[2097152]{0:T(1024)(128)(4,1)S(1)}, s32[]{:S(2)}) async-start(s8[6291456]{0:T(1024)(128)(4,1)} %bitcast.159), calls=%async_computation.14 | async-start | bytes 4194304
  194.6 150.5 %all-reduce.6.cloned.1.call-start = ((), (), s32[]{:S(2)}) async-start(), calls=%async_computation.10 | async-start | bytes 2359296 | tf_op jit(solution)/shard_map/psum | solution.py:234
  223.1 7.1 slice-start
  236.5 4.5 copy-start.26
  243.1 133.0 %reduce-scatter.5.cloned.1.call-start = ((), (), s32[]{:S(2)}) async-start(), calls=%async_computation.9 | async-start | bytes 1966080 | tf_op jit(solution)/shard_map/reduce_scatter | solution.py:223
  247.0 6.3 copy-start.25
  247.0 512.5 %all-reduce.8.cloned.1.call-start = ((), (), s32[]{:S(2)}) async-start(), calls=%async_computation.11 | async-start | bytes 18874368 | tf_op jit(solution)/shard_map/psum | solution.py:161
  261.7 114.4 %copy-start.5 = (bf16[1,256,768]{2,1,0:T(8,128)(2,1)S(1)}, bf16[1,256,768]{2,1,0:T(8,128)(2,1)}, u32[]{:S(2)}) copy-start(bf16[1,256,768]{2,1,0:T(8,128)(2,1)} %param.14) | copy-start | bytes 1179652
  261.7 114.4 %copy-start.29 = (f32[768]{0:T(1024)S(1)}, f32[768]{0:T(1024)}, u32[]{:S(2)}) copy-start(f32[768]{0:T(1024)} %param.20) | copy-start | bytes 9220
  261.7 218.3 %copy-start.10 = (f32[256,768]{1,0:T(8,128)S(1)}, f32[256,768]{1,0:T(8,128)}, u32[]{:S(2)}) copy-start(f32[256,768]{1,0:T(8,128)} %copy-done.9) | copy-start | bytes 2359300
  261.7 218.3 %copy-start.15 = (bf16[1,256,768]{2,1,0:T(8,128)(2,1)S(1)}, bf16[1,256,768]{2,1,0:T(8,128)(2,1)}, u32[]{:S(2)}) copy-start(bf16[1,256,768]{2,1,0:T(8,128)(2,1)} %param.15) | copy-start | bytes 1179652
  759.5 7.5 copy-start.11
  767.0 4.5 copy-start.1
  (16 other events, 39.8 us)
Sparse Core Ops, SparseCore 0:
  11.8 27.9 all-gather.2
  54.6 38.2 reduce-scatter.2
  194.7 26.2 all-gather.4
  243.2 101.8 all-reduce.5
  347.3 28.7 reduce-scatter.4
  379.1 380.3 all-reduce.7
where the time goes:
time: 794 us; the launch traced here: 779 us
  waiting for transfers between devices  494 us (62%)
  blocking collectives  101 us (13%)
  matrix products  79.8 us (10%)
  other arithmetic  42.4 us (5%)
  starting transfers between devices  32.2 us (4%)
  between operations  15.2 us (2%)
  local copies, waits for them, and re-layouts  15.1 us (2%)
    psum x1, waiting for transfers between devices, body(): lax.psum(up_grad.astype(jnp.bfloat16), ('head', 'dp')).astype(jnp.float32)  277 us
    psum x1, blocking collectives, body(): lax.psum((gain_one_grad, gain_two_grad, local_loads), ('head', 'expert',...  101 us
    psum x1, waiting for transfers between devices, body(): lax.psum(joint_weight_grad.astype(jnp.bfloat16), ('expert', 'dp'))  83.4 us
    reduce_scatter x1, waiting for transfers between devices, body(): lax.psum_scatter(jnp.dot(section, w_output, preferred_element_type=jnp.fl...  35.7 us
    reduce_scatter x1, waiting for transfers between devices, body(): lax.psum_scatter(lax.dot_general(section, w_joint, CONTRACT_COLUMNS, pref...  26.8 us
    all_gather x1, waiting for transfers between devices, body(): lax.all_gather(hidden_grad.astype(jnp.bfloat16), 'head', axis=0, tiled=True)  26.3 us
    all_gather x1, waiting for transfers between devices, body(): lax.all_gather(normed_one.astype(jnp.bfloat16), 'head', axis=0, tiled=True)  21.2 us
  transfers between devices with their start and end apart: 10, of which 10 were waited for; matrix products, arithmetic and copies ran while one was open for 7% of the time, Pallas kernels for 0%

commit v1 on v0

v1 whole, which is shorter than its diff:
```python
import functools

import jax
import jax.numpy as jnp
from jax import lax
from jax.experimental import pallas as pl
from jax.experimental.pallas import tpu as pltpu
from jax.sharding import PartitionSpec as P

MESH = pl.DeviceIdType.MESH
f32 = jnp.float32
bf16 = jnp.bfloat16
i32 = jnp.int32

HEADS_X = 4
EXPERTS = 16
TOK = 256
ROW = 1024
D = 768
FF = 3072
CAP = 32
SLOTS = EXPERTS * CAP
WIN = 768
HEAD_COLS = 192
PAD_COLS = 256
FF_CHUNK = 512
EPSILON = 1e-05
NEGATIVE = -1e30
GELU_A = 0.7978845608028654
GELU_B = 0.044715

NN = (((1,), (0,)), ((), ()))
NT = (((1,), (1,)), ((), ()))
TN = (((0,), (0,)), ((), ()))


def dot(a, b, dims=NN):
    return lax.dot_general(a, b, dims, preferred_element_type=f32)


def iota(shape, dim):
    return lax.broadcasted_iota(i32, shape, dim)


def norm_parts(x):
    average = jnp.mean(x, axis=-1, keepdims=True)
    centred = x - average
    variance = jnp.mean(centred * centred, axis=-1, keepdims=True)
    scale = lax.rsqrt(variance + EPSILON)
    return centred * scale, scale


def norm_pull(upstream, normed, scale, gain):
    m = upstream * gain
    first = jnp.mean(m, axis=-1, keepdims=True)
    second = jnp.mean(m * normed, axis=-1, keepdims=True)
    return scale * (m - first - normed * second)


def gelu_pair(u):
    u2 = u * u
    half = 0.5 + 0.5 * jnp.tanh(u * (GELU_A + (GELU_A * GELU_B) * u2))
    slope = half + (u + u) * (half * (1.0 - half)) * (GELU_A + (3.0 * GELU_A * GELU_B) * u2)
    return u * half, slope


def rows(start, size):
    return pl.ds(pl.multiple_of(start, size), size)


def block_kernel(
    tok, og, wq, wk, wv, wo, gain1, gain2, up_hbm, dn_hbm, table, ids, lengths, prompt,
    final, tgrad, gsum, small, x_all, g_all, cnt,
    wj, wjt, gath, qkv, att_snd, att, wo_full, up, dn, snd_a, snd_b, g_own, x_own, gc, xc,
    pack, ag, act, eacc, eg_rcv, out_rcv, disp, disp_t, hid, hgrad, mixed, agr_snd, agr,
    dq, dk, dv, jg, ng_snd, ng_rcv, wog_snd, wog_rcv, gfull, gpart, rs_core, rs_rcv, rs_pair,
    sm_x, sm_e, sm_d,
    load_sem, own_sem, nrm_s, nrm_r, wo_s, wo_r, gd_s, gd_r, xd_s, xd_r, eg_s, eg_r, out_s, out_r,
    att_s, att_r, agr_s, agr_r, ng_s, ng_r, wog_s, wog_r, tg_s, tg_r, tx_s, tx_r, ct_s, ct_r,
    ca_s, ca_r, a2_s, a2_r, a3_s, a3_r, a4_s, a4_r, sx_s, sx_r, se_s, se_r, sd_s, sd_r,
):
    h = lax.axis_index("head")
    e = lax.axis_index("expert")
    d = lax.axis_index("dp")
    right, left, across = lax.rem(h + 1, 4), lax.rem(h + 3, 4), lax.rem(h + 2, 4)
    x_peers = (right, left, across)
    x_from = (left, right, across)
    other = 1 - d
    twin = e + 1 - 2 * lax.rem(e, 2)

    def remote(src, dst, ss, rs, device):
        return pltpu.make_async_remote_copy(
            src_ref=src, dst_ref=dst, send_sem=ss, recv_sem=rs, device_id=device, device_id_type=MESH
        )

    def spread(snd, rcv, ss, rs):
        def step(k, carry):
            p = lax.rem(e + k, EXPERTS)
            remote(
                snd.at[rows(p * CAP, CAP)], rcv.at[rows(e * CAP, CAP)], ss.at[k], rs.at[k], (h, p, d)
            ).start()
            return carry

        lax.fori_loop(1, EXPERTS, step, 0)
        rcv[rows(e * CAP, CAP), :] = snd[rows(e * CAP, CAP), :]

    def spread_recv(snd, rcv, ss, rs):
        def step(k, carry):
            p = lax.rem(e + EXPERTS - k, EXPERTS)
            remote(
                snd.at[rows(p * CAP, CAP)], rcv.at[rows(p * CAP, CAP)], ss.at[k], rs.at[k], (h, p, d)
            ).wait_recv()
            return carry

        lax.fori_loop(1, EXPERTS, step, 0)

    def spread_sent(snd, rcv, ss, rs):
        def step(k, carry):
            p = lax.rem(e + k, EXPERTS)
            remote(
                snd.at[rows(p * CAP, CAP)], rcv.at[rows(e * CAP, CAP)], ss.at[k], rs.at[k], (h, p, d)
            ).wait_send()
            return carry

        lax.fori_loop(1, EXPERTS, step, 0)

    def cross(snd, rcv, ss, rs, only=None):
        view = (lambda r, i: r.at[i]) if only is None else (lambda r, i: r.at[i, pl.ds(0, only)])
        out = [
            remote(view(snd, p), view(rcv, h), ss.at[i], rs.at[i], (p, e, d))
            for i, p in enumerate(x_peers)
        ]
        into = [
            remote(view(snd, p), view(rcv, p), ss.at[i], rs.at[i], (p, e, d))
            for i, p in enumerate(x_from)
        ]
        return out, into

    def gather(buf, ss, rs, only=None):
        view = (lambda r, i: r.at[i]) if only is None else (lambda r, i: r.at[i, pl.ds(0, only)])
        out = [
            remote(view(buf, h), view(buf, h), ss.at[i], rs.at[i], (p, e, d))
            for i, p in enumerate(x_peers)
        ]
        into = [
            remote(view(buf, p), view(buf, p), ss.at[i], rs.at[i], (p, e, d))
            for i, p in enumerate(x_from)
        ]
        return out, into

    def token_copies(own, dst, ss, rs):
        def blk(hh, dd):
            return dd * 4 + hh

        half = pl.ds(0, 256)
        rest = pl.ds(256, 256)
        me = dst.at[blk(h, d)]
        out = [
            remote(own, me, ss.at[0], rs.at[0], (right, e, d)),
            remote(own, me, ss.at[1], rs.at[1], (left, e, d)),
            remote(own, me, ss.at[2], rs.at[2], (h, e, other)),
            remote(
                dst.at[blk(left, d), half], dst.at[blk(left, d), half], ss.at[3], rs.at[3], (right, e, d)
            ),
            remote(
                dst.at[blk(right, d), rest], dst.at[blk(right, d), rest], ss.at[4], rs.at[4], (left, e, d)
            ),
            remote(dst.at[blk(h, other)], dst.at[blk(h, other)], ss.at[5], rs.at[5], (right, e, d)),
            remote(dst.at[blk(h, other)], dst.at[blk(h, other)], ss.at[6], rs.at[6], (left, e, d)),
            remote(dst.at[blk(across, d)], dst.at[blk(across, d)], ss.at[7], rs.at[7], (h, e, other)),
        ]
        places = [
            dst.at[blk(left, d)],
            dst.at[blk(right, d)],
            dst.at[blk(h, other)],
            dst.at[blk(across, d), half],
            dst.at[blk(across, d), rest],
            dst.at[blk(left, other)],
            dst.at[blk(right, other)],
            dst.at[blk(across, other)],
        ]
        senders = [
            (left, e, d), (right, e, d), (h, e, other), (left, e, d),
            (right, e, d), (left, e, d), (right, e, d), (h, e, other),
        ]
        into = [
            remote(p, p, ss.at[i], rs.at[i], s) for i, (p, s) in enumerate(zip(places, senders))
        ]
        return out, into

    g_out, g_into = token_copies(gc, g_all, tg_s, tg_r)
    t_out, t_into = token_copies(xc, x_all, tx_s, tx_r)

    up_load = pltpu.make_async_copy(up_hbm, up, load_sem.at[0])
    dn_load = pltpu.make_async_copy(dn_hbm, dn, load_sem.at[1])
    up_load.start()
    dn_load.start()

    barrier = pltpu.get_barrier_semaphore()
    for p in x_peers:
        pl.semaphore_signal(barrier, inc=1, device_id=(p, e, d), device_id_type=MESH)
    pl.semaphore_signal(barrier, inc=1, device_id=(h, e, other), device_id_type=MESH)

    def greet(k, carry):
        pl.semaphore_signal(
            barrier, inc=1, device_id=(h, lax.rem(e + k, EXPERTS), d), device_id_type=MESH
        )
        return carry

    lax.fori_loop(1, EXPERTS, greet, 0)

    one, _ = norm_parts(tok[...].astype(f32))
    gath[h] = (one * gain1[...]).astype(bf16)
    wj[...] = jnp.zeros_like(wj)
    wj[:, 0:HEAD_COLS] = wq[...]
    wj[:, PAD_COLS : PAD_COLS + HEAD_COLS] = wk[...]
    wj[:, 2 * PAD_COLS : 2 * PAD_COLS + HEAD_COLS] = wv[...]
    for i in range(4):
        wo_full[i, HEAD_COLS:PAD_COLS, :] = jnp.zeros((PAD_COLS - HEAD_COLS, D), bf16)
    wo_full[h, 0:HEAD_COLS, :] = wo[...]

    pl.semaphore_wait(barrier, 3 + 1 + EXPERTS - 1)
    nrm_out, nrm_into = gather(gath, nrm_s, nrm_r)
    for c in nrm_out:
        c.start()

    eye = iota((TOK, TOK), 0) == iota((TOK, TOK), 1)
    id_col = jnp.sum(jnp.where(eye, ids[...].astype(f32), 0.0), axis=1, keepdims=True).astype(i32)
    high, low = lax.shift_right_logical(id_col, 7), lax.bitwise_and(id_col, 127)
    pick = jnp.where(iota((TOK, 256), 1) == high, 1.0, 0.0).astype(bf16)
    near = dot(pick, table[...].astype(f32).astype(bf16))
    lane = iota((TOK, 128), 1)
    chosen = jnp.sum(jnp.where(lane == low, near, 0.0), axis=1, keepdims=True)
    member = jnp.where(lane == chosen.astype(i32), 1.0, 0.0)
    before = jnp.where(iota((TOK, TOK), 1) < iota((TOK, TOK), 0), 1.0, 0.0).astype(bf16)
    rank = jnp.sum(dot(before, member.astype(bf16)) * member, axis=1, keepdims=True)
    slot = chosen * CAP + rank
    slot_row = jnp.sum(jnp.where(eye, slot, 0.0), axis=0, keepdims=True).astype(i32)
    disp_t[...] = jnp.where(iota((TOK, SLOTS), 1) == slot.astype(i32), 1.0, 0.0).astype(bf16)
    disp[...] = jnp.where(iota((SLOTS, TOK), 0) == slot_row, 1.0, 0.0).astype(bf16)
    sm_x[h] = jnp.zeros((8, D), f32)
    sm_x[h, 2:3, 0:128] = jnp.sum(member, axis=0, keepdims=True)

    snd_a[...] = dot(disp[...], og[...]).astype(bf16)
    spread(snd_a, g_own, gd_s, gd_r)

    column_scale = jnp.where(iota((1, D), 1) < PAD_COLS, 0.125, 1.0)

    def project(b):
        qkv[rows(b * TOK, TOK), :] = (dot(gath[b], wj[...]) * column_scale).astype(bf16)

    project(h)
    wo_out, wo_into = gather(wo_full, wo_s, wo_r, HEAD_COLS)
    for i, b in enumerate(x_from):
        nrm_into[i].wait_recv()
        if i == 2:
            for c in wo_out:
                c.start()
        project(b)

    ends = []
    total = 0
    for j in range(8):
        total = total + lengths[0, j]
        ends.append(total)

    def segment(pos):
        found = jnp.zeros(pos.shape, i32)
        for j in range(8):
            found = found + jnp.where(ends[j] <= pos, 1, 0)
        return found

    def window(b):
        first = jnp.minimum(jnp.maximum(b - 1, 0), 1) * TOK
        q_pos = b * TOK + iota((TOK, 1), 0)
        k_pos = first + iota((1, WIN), 1)
        said = prompt[:, pl.ds(pl.multiple_of(first, TOK), WIN)]
        k_least = jnp.where(said == 1, -1, k_pos)
        allowed = (segment(q_pos) == segment(k_pos)) & (k_least <= q_pos)
        return pl.ds(pl.multiple_of(first, TOK), WIN), allowed

    lane_low = iota((TOK, 128), 1) < 64

    def head_mask(head, x):
        if head == 2:
            return x
        return jnp.where(lane_low if head == 0 else jnp.logical_not(lane_low), x, jnp.zeros_like(x))

    def head_lanes(head, part):
        return pl.ds(part * PAD_COLS + (head // 2) * 128, 128)

    def attend(b, carry):
        keys, allowed = window(b)
        mine = rows(b * TOK, TOK)
        groups = [None, None]
        for head in range(3):
            q = head_mask(head, qkv[mine, head_lanes(head, 0)])
            s = dot(q, qkv[keys, head_lanes(head, 1)], NT)
            s = jnp.where(allowed, s, NEGATIVE)
            p = jnp.exp(s - jnp.max(s, axis=-1, keepdims=True))
            total = jnp.sum(p, axis=-1, keepdims=True)
            o = dot(p.astype(bf16), qkv[keys, head_lanes(head, 2)]) * (1.0 / total)
            o = head_mask(head, o)
            g = head // 2
            groups[g] = o if groups[g] is None else groups[g] + o
        att_snd[b, :, 0:128] = groups[0].astype(bf16)
        att_snd[b, :, 128:256] = groups[1].astype(bf16)
        return carry

    lax.fori_loop(0, 4, attend, 0)
    att_out, att_into = cross(att_snd, att, att_s, att_r)
    for c in att_out:
        c.start()
    att[h] = att_snd[h]

    spread_recv(snd_a, g_own, gd_s, gd_r)
    there = jnp.max(jnp.abs(g_own[...].astype(f32)), axis=1, keepdims=True) > 0.0
    there_f = jnp.where(there, 1.0, 0.0)
    earlier = jnp.where(iota((SLOTS, SLOTS), 1) < iota((SLOTS, SLOTS), 0), 1.0, 0.0).astype(bf16)
    place = dot(earlier, jnp.broadcast_to(there_f, (SLOTS, 128)).astype(bf16))[:, 0:1]
    place = jnp.where(there, place, -1.0).astype(i32)
    pack[...] = jnp.where(iota((SLOTS, SLOTS), 1) == place, 1.0, 0.0).astype(bf16)
    gc[...] = dot(pack[...], g_own[...], TN).astype(bf16)
    cnt[d, h] = jnp.broadcast_to(jnp.sum(there_f, axis=0, keepdims=True), (8, 128))
    for i in range(3):
        g_out[i].start()
    g_mine = pltpu.make_async_copy(gc, g_all.at[d * 4 + h], own_sem.at[0])
    g_mine.start()
    c_out = [
        remote(cnt.at[d, h], cnt.at[d, h], ct_s.at[i], ct_r.at[i], (p, e, d))
        for i, p in enumerate(x_peers)
    ]
    c_into = [
        remote(cnt.at[d, p], cnt.at[d, p], ct_s.at[i], ct_r.at[i], (p, e, d))
        for i, p in enumerate(x_from)
    ]
    c_pair = remote(cnt.at[d], cnt.at[d], ct_s.at[3], ct_r.at[3], (h, e, other))
    c_pair_in = remote(cnt.at[other], cnt.at[other], ct_s.at[3], ct_r.at[3], (h, e, other))
    for c in c_out:
        c.start()

    for c in wo_into:
        c.wait_recv()
    for c in att_into:
        c.wait_recv()
    for i in range(4):
        part = dot(att[i], wo_full[i])
        hid[...] = (tok[...].astype(f32) if i == 0 else hid[...]) + part
    two, _ = norm_parts(hid[...])
    snd_b[...] = dot(disp[...], (two * gain2[...]).astype(bf16)).astype(bf16)
    spread(snd_b, x_own, xd_s, xd_r)

    for c in c_into:
        c.wait_recv()
    c_pair.start()
    dn_load.wait()

    def back_down(c, carry):
        part = pl.ds(pl.multiple_of(c * FF_CHUNK, FF_CHUNK), FF_CHUNK)
        ag[:, part] = dot(g_own[...], dn[part, :], NT)
        return carry

    lax.fori_loop(0, FF // FF_CHUNK, back_down, 0)
    up_load.wait()
    for i in range(2):
        g_into[i].wait_recv()
    g_out[3].start()
    g_out[4].start()
    g_into[2].wait_recv()
    g_out[5].start()
    g_out[6].start()
    spread_sent(snd_a, g_own, gd_s, gd_r)
    spread_recv(snd_b, x_own, xd_s, xd_r)

    eacc[...] = jnp.zeros_like(eacc)

    def expert(c, carry):
        part = pl.ds(pl.multiple_of(c * FF_CHUNK, FF_CHUNK), FF_CHUNK)
        value, slope = gelu_pair(dot(x_own[...], up[:, part]))
        act[:, part] = value.astype(bf16)
        pre_grad = (ag[:, part] * slope).astype(bf16)
        eacc[...] += dot(pre_grad, up[:, part], NT)
        return carry

    lax.fori_loop(0, FF // FF_CHUNK, expert, 0)
    snd_a[...] = eacc[...].astype(bf16)
    spread(snd_a, eg_rcv, eg_s, eg_r)
    xc[...] = dot(pack[...], x_own[...], TN).astype(bf16)
    spread_sent(snd_b, x_own, xd_s, xd_r)
    eacc[...] = jnp.zeros_like(eacc)

    def produce(c, carry):
        part = pl.ds(pl.multiple_of(c * FF_CHUNK, FF_CHUNK), FF_CHUNK)
        eacc[...] += dot(act[:, part], dn[part, :])
        return carry

    lax.fori_loop(0, FF // FF_CHUNK, produce, 0)
    snd_b[...] = eacc[...].astype(bf16)
    spread(snd_b, out_rcv, out_s, out_r)
    for i in range(3):
        t_out[i].start()
    x_mine = pltpu.make_async_copy(xc, x_all.at[d * 4 + h], own_sem.at[1])
    x_mine.start()
    g_into[3].wait_recv()
    g_into[4].wait_recv()
    g_out[7].start()
    wjt[...] = wj[...].astype(f32).T
    spread_recv(snd_a, eg_rcv, eg_s, eg_r)

    two, scale2 = norm_parts(hid[...])
    back = dot(disp_t[...], eg_rcv[...])
    sm_x[h, 1:2, :] = jnp.sum(back * two, axis=0, keepdims=True)
    hgrad[...] = og[...].astype(f32) + norm_pull(back, two, scale2, gain2[...])
    mixed[...] = hgrad[...].astype(bf16)

    def back_output(i, carry):
        agr_snd[i] = dot(mixed[...], wo_full[i], NT).astype(bf16)
        return carry

    lax.fori_loop(0, 4, back_output, 0)
    agr_out, agr_into = cross(agr_snd, agr, agr_s, agr_r)
    for c in agr_out:
        c.start()
    agr[h] = agr_snd[h]

    def output_grad(i, carry):
        wog_snd[i] = dot(att[i], mixed[...], TN).astype(bf16)
        return carry

    lax.fori_loop(0, 4, output_grad, 0)
    wog_out, wog_into = cross(wog_snd, wog_rcv, wog_s, wog_r, HEAD_COLS)
    for c in wog_out:
        c.start()
    dq[...] = jnp.zeros_like(dq)
    dk[...] = jnp.zeros_like(dk)
    dv[...] = jnp.zeros_like(dv)
    for c in agr_into:
        c.wait_recv()

    def attend_back(b, carry):
        keys, allowed = window(b)
        mine = rows(b * TOK, TOK)
        for head in range(3):
            g = pl.ds((head // 2) * 128, 128)
            q = head_mask(head, qkv[mine, head_lanes(head, 0)])
            k = qkv[keys, head_lanes(head, 1)]
            v = qkv[keys, head_lanes(head, 2)]
            u = head_mask(head, agr[b, :, g])
            s = jnp.where(allowed, dot(q, k, NT), NEGATIVE)
            p = jnp.exp(s - jnp.max(s, axis=-1, keepdims=True))
            chances = p * (1.0 / jnp.sum(p, axis=-1, keepdims=True))
            chance_grad = dot(u, v, NT)
            inner = jnp.sum(chance_grad * chances, axis=-1, keepdims=True)
            score_grad = (chances * (chance_grad - inner)).astype(bf16)
            dq[mine, g] += head_mask(head, dot(score_grad, k)) * 0.125
            dk[keys, g] += dot(score_grad, q, TN)
            dv[keys, g] += dot(chances.astype(bf16), u, TN)
        return carry

    lax.fori_loop(0, 4, attend_back, 0)
    jg[:, 0:PAD_COLS] = dq[...].astype(bf16)
    jg[:, PAD_COLS : 2 * PAD_COLS] = dk[...].astype(bf16)
    jg[:, 2 * PAD_COLS : 3 * PAD_COLS] = dv[...].astype(bf16)

    ng_out, ng_into = cross(ng_snd, ng_rcv, ng_s, ng_r)
    for i, p in enumerate((across, right, left)):
        ng_snd[p] = dot(jg[rows(p * TOK, TOK), :], wj[...], NT).astype(bf16)
        ng_out[(2, 0, 1)[i]].start()

    for c in wog_into:
        c.wait_recv()
    wog = wog_snd[h, 0:HEAD_COLS, :].astype(f32)
    for p in x_from:
        wog = wog + wog_rcv[p, 0:HEAD_COLS, :].astype(f32)
    gfull[3 * HEAD_COLS : 4 * HEAD_COLS, :] = wog.astype(bf16)
    gain1_part = jnp.zeros((1, D), f32)
    for part in range(3):
        grad = jnp.zeros((PAD_COLS, D), f32)
        for b in range(4):
            grad = grad + dot(jg[b * TOK : (b + 1) * TOK, part * PAD_COLS : (part + 1) * PAD_COLS], gath[b], TN)
        gain1_part = gain1_part + jnp.sum(
            grad * wjt[part * PAD_COLS : (part + 1) * PAD_COLS, :], axis=0, keepdims=True
        )
        gfull[part * HEAD_COLS : (part + 1) * HEAD_COLS, :] = grad[0:HEAD_COLS, :].astype(bf16)
    sm_x[h, 0:1, :] = gain1_part / gain1[...]

    core = lax.rem(e, 2)
    mine_half = rows(core * 384, 384)
    twin_half = rows((1 - core) * 384, 384)
    ca_out = remote(gfull.at[twin_half], rs_core, ca_s.at[0], ca_r.at[0], (h, twin, d))
    ca_out.start()
    sx_out, sx_into = gather(sm_x, sx_s, sx_r)
    for c in sx_out:
        c.start()

    own_grad = dot(jg[rows(h * TOK, TOK), :], wj[...], NT)
    ca_out.wait_recv()
    gpart[...] = (gfull[mine_half, :].astype(f32) + rs_core[...].astype(f32)).astype(bf16)

    unit = lax.div(e, 2)

    def peer(k):
        return lax.rem(unit + k, 8)

    def a2_copy(k, where):
        p = peer(k)
        return remote(
            gpart.at[rows(p * 48, 48)], rs_rcv.at[where], a2_s.at[k], a2_r.at[k], (h, p * 2 + core, d)
        )

    for k in range(1, 8):
        a2_copy(k, unit).start()
    rs_rcv[unit] = gpart[rows(unit * 48, 48), :]
    for c in sx_into:
        c.wait_recv()
    sm_e[e] = (sm_x[0] + sm_x[1]) + (sm_x[2] + sm_x[3])

    def small_copy(k, p, where):
        return remote(sm_e.at[e], sm_e.at[where], se_s.at[k], se_r.at[k], (h, p, d))

    def small_start(k, carry):
        p = lax.rem(e + k, EXPERTS)
        small_copy(k, p, e).start()
        return carry

    lax.fori_loop(1, EXPERTS, small_start, 0)

    for c in ng_into:
        c.wait_recv()
    for p in x_from:
        own_grad = own_grad + ng_rcv[p].astype(f32)
    one, scale1 = norm_parts(tok[...].astype(f32))
    tgrad[...] = hgrad[...] + norm_pull(own_grad, one, scale1, gain1[...])

    for k in range(1, 8):
        a2_copy(k, peer(8 - k)).wait_recv()
    reduced = rs_rcv[0].astype(f32)
    for k in range(1, 8):
        reduced = reduced + rs_rcv[k].astype(f32)
    rs_pair[d] = reduced.astype(bf16)
    a3 = remote(rs_pair.at[d], rs_pair.at[d], a3_s.at[0], a3_r.at[0], (h, e, other))
    a3_in = remote(rs_pair.at[other], rs_pair.at[other], a3_s.at[0], a3_r.at[0], (h, e, other))
    a3.start()

    def small_recv(k, carry):
        p = lax.rem(e + EXPERTS - k, EXPERTS)
        small_copy(k, p, p).wait_recv()
        return carry

    lax.fori_loop(1, EXPERTS, small_recv, 0)
    gathered = sm_e[0]
    for k in range(1, EXPERTS):
        gathered = gathered + sm_e[k]
    sm_d[d] = gathered
    sd = remote(sm_d.at[d], sm_d.at[d], sd_s.at[0], sd_r.at[0], (h, e, other))
    sd_in = remote(sm_d.at[other], sm_d.at[other], sd_s.at[0], sd_r.at[0], (h, e, other))
    sd.start()

    spread_recv(snd_b, out_rcv, out_s, out_r)
    final[...] = hid[...] + dot(disp_t[...], out_rcv[...])

    a3_in.wait_recv()
    here = rows(core * 384 + unit * 48, 48)
    gsum[here, :] = (rs_pair[0].astype(f32) + rs_pair[1].astype(f32)).astype(bf16)

    def a4_copy(k, p, place):
        return remote(gsum.at[place], gsum.at[place], a4_s.at[k], a4_r.at[k], (h, p * 2 + core, d))

    for k in range(1, 8):
        a4_copy(k, peer(k), here).start()

    for i in range(2):
        t_into[i].wait_recv()
    t_out[3].start()
    t_out[4].start()
    t_into[2].wait_recv()
    t_out[5].start()
    t_out[6].start()
    sd_in.wait_recv()
    small[...] = sm_d[0] + sm_d[1]
    for k in range(1, 8):
        p = peer(8 - k)
        a4_copy(k, p, rows(core * 384 + p * 48, 48)).wait_recv()
    for k in range(1, 8):
        a4_copy(k, peer(k), here).wait_send()
    a5 = remote(gsum.at[mine_half], gsum.at[mine_half], ca_s.at[1], ca_r.at[1], (h, twin, d))
    a5_in = remote(gsum.at[twin_half], gsum.at[twin_half], ca_s.at[1], ca_r.at[1], (h, twin, d))
    a5.start()
    a5_in.wait_recv()
    t_into[3].wait_recv()
    t_into[4].wait_recv()
    t_out[7].start()
    for i in range(5, 8):
        g_into[i].wait_recv()
        t_into[i].wait_recv()
    c_pair_in.wait_recv()

    g_mine.wait()
    x_mine.wait()
    spread_sent(snd_a, eg_rcv, eg_s, eg_r)
    spread_sent(snd_b, out_rcv, out_s, out_r)

    def small_sent(k, carry):
        p = lax.rem(e + k, EXPERTS)
        small_copy(k, p, e).wait_send()
        return carry

    lax.fori_loop(1, EXPERTS, small_sent, 0)
    for k in range(1, 8):
        a2_copy(k, unit).wait_send()
    for c in (
        nrm_out + wo_out + att_out + g_out + t_out + c_out + [c_pair] + agr_out + wog_out + ng_out
        + sx_out + [ca_out, a5, a3, sd]
    ):
        c.wait_send()


def block_call(*args):
    vmem = pl.BlockSpec(memory_space=pltpu.VMEM)
    hbm = pl.BlockSpec(memory_space=pl.ANY)
    smem = pl.BlockSpec(memory_space=pltpu.SMEM)
    dma = pltpu.SemaphoreType.DMA

    def buf(*shape, dtype=bf16):
        return pltpu.VMEM(shape, dtype)

    scratch = [
        buf(D, D), buf(D, D, dtype=f32), buf(4, TOK, D), buf(ROW, D), buf(4, TOK, PAD_COLS), buf(4, TOK, PAD_COLS),
        buf(4, PAD_COLS, D), buf(D, FF), buf(FF, D), buf(SLOTS, D), buf(SLOTS, D), buf(SLOTS, D),
        buf(SLOTS, D), buf(SLOTS, D), buf(SLOTS, D),
        buf(SLOTS, SLOTS), buf(SLOTS, FF, dtype=f32), buf(SLOTS, FF), buf(SLOTS, D, dtype=f32),
        buf(SLOTS, D), buf(SLOTS, D), buf(SLOTS, TOK), buf(TOK, SLOTS),
        buf(TOK, D, dtype=f32), buf(TOK, D, dtype=f32), buf(TOK, D), buf(4, TOK, PAD_COLS), buf(4, TOK, PAD_COLS),
        buf(ROW, PAD_COLS, dtype=f32), buf(ROW, PAD_COLS, dtype=f32), buf(ROW, PAD_COLS, dtype=f32),
        buf(ROW, D), buf(4, TOK, D), buf(4, TOK, D), buf(4, PAD_COLS, D), buf(4, PAD_COLS, D),
        buf(D, D), buf(384, D), buf(384, D), buf(8, 48, D), buf(2, 48, D),
        buf(4, 8, D, dtype=f32), buf(EXPERTS, 8, D, dtype=f32), buf(2, 8, D, dtype=f32),
        dma((2,)), dma((2,)),
    ]
    for n in (3, 3, 16, 16, 16, 16, 3, 3, 3, 3, 8, 8, 4, 2, 8, 1, 8, 3, 16, 1):
        scratch += [dma((n,)), dma((n,))]
    return pl.pallas_call(
        block_kernel,
        out_shape=[
            jax.ShapeDtypeStruct((TOK, D), f32),
            jax.ShapeDtypeStruct((TOK, D), f32),
            jax.ShapeDtypeStruct((D, D), bf16),
            jax.ShapeDtypeStruct((8, D), f32),
            jax.ShapeDtypeStruct((8, SLOTS, D), bf16),
            jax.ShapeDtypeStruct((8, SLOTS, D), bf16),
            jax.ShapeDtypeStruct((2, 4, 8, 128), f32),
        ],
        in_specs=[vmem] * 8 + [hbm, hbm, vmem, vmem, smem, vmem],
        out_specs=[vmem] * 4 + [hbm, hbm, vmem],
        scratch_shapes=scratch,
        compiler_params=pltpu.CompilerParams(
            collective_id=1, has_side_effects=True, vmem_limit_bytes=64 * 2**20 - 2**16
        ),
    )(*args)


GRAD_TILE = 512
REST_TILE = 256


def expert_grad_kernel(n_ref, x_ref, g_ref, up_ref, dn_ref, du_ref, dd_ref, xs, gs):
    total = 0
    ends = []
    for b in range(8):
        ends.append(total)
        total = total + lax.div(n_ref[b] + 15, 16) * 16

    @pl.when(pl.program_id(0) == 0)
    def _():
        for b in range(8):
            there = pl.ds(pl.multiple_of(ends[b], 16), SLOTS)
            xs[there, :] = x_ref[b]
            gs[there, :] = g_ref[b]
        tail = pl.ds(pl.multiple_of(total, 16), SLOTS)
        xs[tail, :] = jnp.zeros((SLOTS, D), bf16)
        gs[tail, :] = jnp.zeros((SLOTS, D), bf16)

    du_ref[...] = jnp.zeros_like(du_ref)
    dd_ref[...] = jnp.zeros_like(dd_ref)

    def tile(start, size):
        r = pl.ds(pl.multiple_of(start, size), size)
        x, g = xs[r, :], gs[r, :]
        value, slope = gelu_pair(dot(x, up_ref[...]))
        pre_grad = (dot(g, dn_ref[...], NT) * slope).astype(bf16)
        du_ref[...] += dot(x, pre_grad, TN)
        dd_ref[...] += dot(value.astype(bf16), g, TN)

    def whole(i, carry):
        tile(i * GRAD_TILE, GRAD_TILE)
        return carry

    def rest(i, carry):
        tile(i * REST_TILE, REST_TILE)
        return carry

    full = lax.div(total, GRAD_TILE)
    lax.fori_loop(0, full, whole, 0)
    lax.fori_loop(full * (GRAD_TILE // REST_TILE), lax.div(total + REST_TILE - 1, REST_TILE), rest, 0)


def expert_grads(counts, x_all, g_all, up, dn):
    return pl.pallas_call(
        expert_grad_kernel,
        grid_spec=pltpu.PrefetchScalarGridSpec(
            num_scalar_prefetch=1,
            grid=(FF // FF_CHUNK,),
            in_specs=[
                pl.BlockSpec((8, SLOTS, D), lambda i, n: (0, 0, 0)),
                pl.BlockSpec((8, SLOTS, D), lambda i, n: (0, 0, 0)),
                pl.BlockSpec((D, FF_CHUNK), lambda i, n: (0, i)),
                pl.BlockSpec((FF_CHUNK, D), lambda i, n: (i, 0)),
            ],
            out_specs=[
                pl.BlockSpec((D, FF_CHUNK), lambda i, n: (0, i)),
                pl.BlockSpec((FF_CHUNK, D), lambda i, n: (i, 0)),
            ],
            scratch_shapes=[
                pltpu.VMEM((9 * SLOTS, D), bf16),
                pltpu.VMEM((9 * SLOTS, D), bf16),
            ],
        ),
        out_shape=[jax.ShapeDtypeStruct((D, FF), f32), jax.ShapeDtypeStruct((FF, D), f32)],
        compiler_params=pltpu.CompilerParams(vmem_limit_bytes=64 * 2**20 - 2**16),
    )(counts, x_all, g_all, up, dn)


def body(
    tokens, out_grad, w_query, w_key, w_value, w_output, gain_one, gain_two, expert_up, expert_down,
    hash_table, token_ids, doc_lengths, turn_mask,
):
    final, tokens_grad, gsum, small, x_all, g_all, cnt = block_call(
        tokens[0], out_grad[0], w_query, w_key, w_value, w_output,
        gain_one.reshape(1, D), gain_two.reshape(1, D), expert_up[0], expert_down[0],
        hash_table.reshape(256, 128), token_ids, doc_lengths, turn_mask,
    )
    counts = cnt[:, :, 0, 0].reshape(8).astype(i32)
    up_grad, down_grad = expert_grads(counts, x_all, g_all, expert_up[0], expert_down[0])
    grads = gsum.astype(f32)
    return (
        final[None],
        tokens_grad[None],
        grads[0:HEAD_COLS].T,
        grads[HEAD_COLS : 2 * HEAD_COLS].T,
        grads[2 * HEAD_COLS : 3 * HEAD_COLS].T,
        grads[3 * HEAD_COLS :],
        small[0],
        small[1],
        up_grad[None],
        down_grad[None],
        small[2, :EXPERTS].astype(i32),
    )


def solution(mesh):
    rows_spec = P(("expert", "dp"), "head", None)
    in_specs = (
        rows_spec, rows_spec, P(None, "head"), P(None, "head"), P(None, "head"), P("head", None),
        P(), P(), P("expert", None, None), P("expert", None, None), P(),
        P(("expert", "dp"), "head"), P(("expert", "dp"), None), P(("expert", "dp"), None),
    )
    out_specs = (
        rows_spec, rows_spec, P(None, "head"), P(None, "head"), P(None, "head"), P("head", None),
        P(), P(), P("expert", None, None), P("expert", None, None), P(),
    )
    return jax.shard_map(body, mesh=mesh, in_specs=in_specs, out_specs=out_specs, check_vma=False)
```

time: 794 us -> 279 us (0.35); the launches traced: 779 us -> 279 us
  waiting for transfers between devices: 494 us -> 0 us
  Pallas kernels: 0 us -> 260 us
  blocking collectives: 101 us -> 0 us
  matrix products: 79.8 us -> 0 us
  other arithmetic: 42.4 us -> 3.77 us
  starting transfers between devices: 32.2 us -> 0 us
  between operations: 15.2 us -> 0.68 us
    psum x2 -> x0, waiting for transfers between devices: 361 us -> none  [the longest x1 277 us: body(): lax.psum(up_grad.astype(jnp.bfloat16), ('head', 'dp')).astype(jnp.float32)]
    pallas_call x0 -> x2, Pallas kernels: none -> 260 us  [the longest x1 191 us: block_call(): pl.pallas_call(block_kernel, out_shape=[jax.ShapeDtypeStruct((TOK, D), f3...]
    psum x1 -> x0, blocking collectives: 101 us -> none  [body(): lax.psum((gain_one_grad, gain_two_grad, local_loads), ('head', 'expert',...]
    dot_general x24 -> x0, matrix products: 79.8 us -> none  [the longest x1 8.88 us: body(): lax.dot_general(grad_slots, down_weight, CONTRACT_COLUMNS, preferred_elem...]
    reduce_scatter x2 -> x0, waiting for transfers between devices: 62.5 us -> none  [the longest x1 35.7 us: body(): lax.psum_scatter(jnp.dot(section, w_output, preferred_element_type=jnp.fl...]
    all_gather x2 -> x0, waiting for transfers between devices: 47.5 us -> none  [the longest x1 26.3 us: body(): lax.all_gather(hidden_grad.astype(jnp.bfloat16), 'head', axis=0, tiled=True)]
    all_to_all x4 -> x0, starting transfers between devices: 31.5 us -> none  [the longest x1 8.03 us: body(): lax.all_to_all(produced.reshape(expert_count, capacity, width), 'expert',...]
    all_to_all x4 -> x0, waiting for transfers between devices: 22.8 us -> none  [the longest x1 8.86 us: body(): lax.all_to_all(produced.reshape(expert_count, capacity, width), 'expert',...]
  transfers between devices with their start and end apart: 10 -> 0, of which waited for: 10 -> 0; matrix products, arithmetic and copies ran while one was open for 7% -> 0% of each run, Pallas kernels for 0% -> 0%
where the time goes in v1:
time: 279 us
  Pallas kernels  260 us (93%)
  local copies, waits for them, and re-layouts  14.1 us (5%)
  other arithmetic  3.77 us (1%)
    pallas_call x1, Pallas kernels, block_call(): pl.pallas_call(block_kernel, out_shape=[jax.ShapeDtypeStruct((TOK, D), f3...  191 us
    pallas_call x1, Pallas kernels, expert_grads(): pl.pallas_call(expert_grad_kernel, grid_spec=pltpu.PrefetchScalarGridSpec...  69.1 us
    unnamed x11, local copies, waits for them, and re-layouts  7.41 us

profile of v1, /device:TPU:80, one launch (start us, length us, event | category | flops | bytes accessed | tf_op | source)
XLA Modules:
  0.0 278.8 jit_solution(14612834299777741651)
XLA Ops:
  0.6 1.9 copy.28.wq
  2.5 1.9 copy.29.wk
  4.4 1.9 copy.30.wv
  6.3 1.3 reshape.33.gain1
  7.5 1.3 reshape.34.gain2
  8.8 191.2 %shard_map.221 = (f32[256,768]{1,0:T(8,128)}, f32[256,768]{1,0:T(8,128)}, bf16[768,768]{1,0:T(8,128)(2,1)}, f32[8,768]{1,0:T(8,128)}, bf16[8,512,768]{2,1,0:T(8,...) custom-call(bf16[256,768]{1,0:T(8,128)(2,1)} %bitcast.23, bf16[256,768]{1,0:T(8,128)(2,1)} %bitcast.24, ...), custom_call_target="tpu_custom_call" | custom-call | tf_op jit(solution)/shard_map/pallas_call | solution.py:642
  200.0 1.0 convert_reduce_fusion
  201.0 0.6 convert_element_type.16.n_ref
  201.6 69.1 %shard_map.222 = (f32[768,3072]{1,0:T(8,128)}, f32[3072,768]{1,0:T(8,128)}) custom-call(s32[8]{0:T(128)} %convert_element_type.16.n_ref, bf16[8,512,768]{2,1,0:T(8,128)(2,1)} %get-tuple-element.25.x_ref, bf16[8,512,768]{2,1,0:T(8,128)(2,1)} %get-tuple-element.26.g_ref, bf16[768,3072]{1,0:T(8,128)(2,1)} %bitcast.18, bf16[3072,768]{1,0:T(8,128)(2,1)} %bitcast.20), custom_call_target="tpu_custom_call" | custom-call | tf_op jit(solution)/shard_map/pallas_call | solution.py:708
  270.7 0.0 copy-start
  270.7 0.0 copy-start.2
  270.7 0.0 copy-start.1
  270.7 1.6 convert_element_type.14
  272.3 1.2 slice_bitcast_fusion
  273.6 1.4 slice_reduce_fusion
  275.0 0.0 copy-done
  275.0 0.9 slice.35
  275.9 1.2 convert_bitcast_fusion
  277.1 0.0 copy-done.2
  277.1 0.9 copy.33
  277.9 0.0 copy-done.1
  277.9 0.9 copy.34
Async XLA Ops:
  270.7 4.3 %copy-start = (bf16[768,768]{1,0:T(8,128)(2,1)S(1)}, bf16[768,768]{1,0:T(8,128)(2,1)}, u32[]{:S(2)}) copy-start(bf16[768,768]{1,0:T(8,128)(2,1)} %get-tuple-element.22) | copy-start | bytes 3538948
  270.7 6.3 %copy-start.2 = (f32[256,768]{1,0:T(8,128)S(1)}, f32[256,768]{1,0:T(8,128)}, u32[]{:S(2)}) copy-start(f32[256,768]{1,0:T(8,128)} %get-tuple-element.20) | copy-start | bytes 2359300
  270.7 7.2 %copy-start.1 = (f32[256,768]{1,0:T(8,128)S(1)}, f32[256,768]{1,0:T(8,128)}, u32[]{:S(2)}) copy-start(f32[256,768]{1,0:T(8,128)} %get-tuple-element.21) | copy-start | bytes 2359300
